TPU v7x, 256 devices: a whole 4x4x8 slice. The times are simulated.
256 devices in a mesh: outer: 8 (over x, core), inner: 32 (over y, z).
Axes of the slice: x: 4, y: 4, z: 8, core: 2. Of those that a mesh axis runs over, the one named last changes fastest.
Arguments:
- features: bfloat16 [1048576, 512], P(('outer', 'inner'))
- targets: bfloat16 [1048576, 256], P(('outer', 'inner'))
- signs: int32 [1048576], P(('outer', 'inner')), may hold values from 0 to 1
- picks: int32 [262144], P(('outer', 'inner')), may hold values from 0 to 4095, as said below
- routes: int32 [262144], P(('outer', 'inner')), may hold values from 0 to 31, as said below
Outputs:
- sketch: bfloat16 [262144, 768], P(('outer', 'inner'))
- weights: float32 [512, 256], replicated
- predictions: bfloat16 [1048576, 256], P(('outer', 'inner'))
Inputs may be any that keep to these rules, and one draw needn't show every extreme that they name: `signs`: row sign is 2 s - 1. `picks`: the 1024 entries of one block are distinct positions of that block. `routes`: among the 1024 entries of one block every value occurs exactly 32 times.
All inputs are finite; a program needn't handle non-finite values.
Results may differ from a plain program's by a relative error of at most 0.003.
The roundings to bfloat16 on the way count: a program that leaves them out, or rounds other values in their place, can miss the bound.
Values may be sent and summed in bfloat16 or wider, within the bound.
A program may use at most 64 MiB of HBM per device.

v0:
```python
import math

import jax
import jax.numpy as jnp
from jax import lax
from jax.sharding import PartitionSpec as P

SIDE = 64


def hadamard(order):
    matrix = jnp.ones((1, 1), jnp.float32)
    while matrix.shape[0] < order:
        matrix = jnp.concatenate(
            [jnp.concatenate([matrix, matrix], 1), jnp.concatenate([matrix, -matrix], 1)], 0
        )
    return matrix


def mix_sources(received):
    order = received.shape[0]
    mixer = hadamard(order)
    mixed = jnp.einsum(
        "rs,stc->rtc", mixer, received.astype(jnp.float32), precision=lax.Precision.HIGHEST
    ) / math.sqrt(order)
    return mixed.astype(jnp.bfloat16)


def per_device(features, targets, signs, picks, routes):
    feat_width = features.shape[1]
    total_width = feat_width + targets.shape[1]
    block_rows = features.shape[0]
    kept_rows = picks.shape[0]
    inner_count = lax.axis_size("inner")
    factor = hadamard(SIDE)
    rows = jnp.concatenate([features, targets], 1)
    signed = rows * (2 * signs - 1).astype(jnp.bfloat16)[:, None]
    half = jnp.einsum(
        "bj,ijc->ibc",
        factor.astype(jnp.bfloat16),
        signed.reshape(SIDE, SIDE, total_width),
        preferred_element_type=jnp.float32,
    )
    whole = jnp.einsum("ai,ibc->abc", factor, half, precision=lax.Precision.HIGHEST) / SIDE
    kept = whole.reshape(block_rows, total_width)[picks].astype(jnp.bfloat16)
    order = jnp.argsort(routes, stable=True)
    sectioned = kept[order].reshape(inner_count, kept_rows // inner_count, total_width)
    sketch = mix_sources(
        lax.all_to_all(sectioned, "inner", split_axis=0, concat_axis=0, tiled=True)
    ).reshape(kept_rows, total_width)
    gram = jnp.dot(sketch[:, :feat_width].T, sketch, preferred_element_type=jnp.float32)
    total = lax.psum(gram, ("outer", "inner"))
    final_lower = jnp.linalg.cholesky(total[:, :feat_width])
    middle = lax.linalg.triangular_solve(
        final_lower, total[:, feat_width:], left_side=True, lower=True
    )
    weights = lax.linalg.triangular_solve(
        final_lower, middle, left_side=True, lower=True, transpose_a=True
    )
    predictions = jnp.dot(
        features, weights.astype(jnp.bfloat16), preferred_element_type=jnp.float32
    ).astype(jnp.bfloat16)
    return (sketch, weights, predictions)


def solution(mesh):
    in_specs = (
        P(("outer", "inner"), None),
        P(("outer", "inner"), None),
        P(("outer", "inner")),
        P(("outer", "inner")),
        P(("outer", "inner")),
    )
    out_specs = (P(("outer", "inner"), None), P(), P(("outer", "inner"), None))
    return jax.shard_map(
        per_device, mesh=mesh, in_specs=in_specs, out_specs=out_specs, check_vma=False
    )
```

profile of v0, /device:TPU:1, one launch (start us, length us, event | category | flops | bytes accessed | tf_op | source)
XLA Modules:
  0.0 518.9 jit_solution(266586914904309688)
XLA Ops:
  8.0 4.1 fusion.6
  12.1 16.6 %broadcast_multiply_fusion = bf16[64,64,768]{2,0,1:T(8,128)(2,1)S(1)} fusion(f32[64,64,1]{1,0,2:T(8,128)S(1)} %copy-done.5, f32[64,64,768]{2,1,0:T(8,128)S(1)} %fusion.6), kind=kOutput, calls=%fused_computation.10 | convolution fusion | flops 2422210560 | bytes 18890752 | tf_op jit(solution)/shard_map/ai,ibc->abc/dot_general | solution.py:44
  28.7 6.2 %copy.18 = bf16[64,64,768]{2,1,0:T(8,128)(2,1)} copy(bf16[64,64,768]{2,0,1:T(8,128)(2,1)S(1)} %broadcast_multiply_fusion) | data formatting | bytes 12582912 | tf_op jit(solution)/shard_map/div | solution.py:44
  34.9 4.4 sort.17
  39.3 8.1 %gather_fusion = bf16[1024,768]{1,0:T(8,128)(2,1)S(1)} fusion(bf16[4096,768]{1,0:T(8,128)(2,1)} %bitcast.74, s32[1024]{0:T(1024)S(1)} %fusion.57), kind=kCustom, calls=%fused_computation | custom fusion | bytes 3149824 | tf_op jit(solution)/shard_map/gather | solution.py:45
  47.4 4.3 gather_fusion.1
  51.7 48.5 %all_to_all.5 = bf16[32,32,768]{2,1,0:T(8,128)(2,1)S(1)} all-to-all(bf16[32,32,768]{2,1,0:T(8,128)(2,1)S(1)} %bitcast.76), channel_id=1, replica_groups=mesh['outer'=8,'inner'=32] {'inner'}, dimensions={0} | all-to-all | bytes 3145728 | tf_op jit(solution)/shard_map/all_to_all | solution.py:49
  100.3 2.3 multiply_convert_fusion
  103.5 1.1 copy-done.4
  104.6 2.2 fusion.11
  106.8 257.7 %all-reduce.3.cloned.1.call-done = f32[512,768]{0,1:T(8,128)} async-done(((f32[512,768]{0,1:T(8,128)}), f32[512,768]{0,1:T(8,128)}) %all-reduce.3.cloned.1.call-update) | async-done | bytes 1572880 | tf_op jit(solution)/shard_map/psum | solution.py:52
  364.5 1.2 slice-done
  365.7 1.3 copy.22
  367.0 1.4 fusion.13
  368.5 11.7 %cholesky.104 = f32[128,128]{1,0:T(8,128)S(1)} custom-call(f32[128,128]{1,0:T(8,128)S(1)} %cholesky.266), custom_call_target="Cholesky" | custom-call | tf_op jit(solution)/shard_map/jit(cholesky)/cholesky | solution.py:53
  380.2 9.8 %custom-call.32 = f32[1,128,128]{1,2,0:T(8,128)S(1)} custom-call(f32[1,128,128]{2,1,0:T(8,128)S(1)} %get-tuple-element.41), custom_call_target="InvertDiagBlocksLowerTriangular" | custom-call | tf_op jit(solution)/shard_map/jit(cholesky)/cholesky | solution.py:53
  390.8 11.8 %cholesky.217 = f32[128,128]{1,0:T(8,128)S(1)} custom-call(f32[128,128]{1,0:T(8,128)S(1)} %cholesky.270), custom_call_target="Cholesky" | custom-call | tf_op jit(solution)/shard_map/jit(cholesky)/cholesky | solution.py:53
  402.7 9.8 %custom-call.33 = f32[1,128,128]{1,2,0:T(8,128)S(1)} custom-call(f32[1,128,128]{2,1,0:T(8,128)S(1)} %get-tuple-element.38), custom_call_target="InvertDiagBlocksLowerTriangular" | custom-call | tf_op jit(solution)/shard_map/jit(cholesky)/cholesky | solution.py:53
  413.2 11.7 %cholesky.238 = f32[128,128]{1,0:T(8,128)S(1)} custom-call(f32[128,128]{1,0:T(8,128)S(1)} %cholesky.275), custom_call_target="Cholesky" | custom-call | tf_op jit(solution)/shard_map/jit(cholesky)/cholesky | solution.py:53
  425.6 9.8 %custom-call.34 = f32[1,128,128]{1,2,0:T(8,128)S(1)} custom-call(f32[1,128,128]{2,1,0:T(8,128)S(1)} %get-tuple-element.35), custom_call_target="InvertDiagBlocksLowerTriangular" | custom-call | tf_op jit(solution)/shard_map/jit(cholesky)/cholesky | solution.py:53
  436.2 11.7 %cholesky.255 = f32[128,128]{1,0:T(8,128)S(1)} custom-call(f32[128,128]{1,0:T(8,128)S(1)} %convolution_subtract_fusion.8), custom_call_target="Cholesky" | custom-call | tf_op jit(solution)/shard_map/jit(cholesky)/cholesky | solution.py:53
  452.0 7.9 %while.1 = (s32[]{:T(128)}, f32[512,512]{1,0:T(8,128)S(1)}, s32[4,2]{0,1:T(2,128)S(1)}, f32[4,128,128]{2,1,0:T(8,128)S(1)}, s32[]{:T(128)}) while((s32[]{:T(128)}, f32[512,512]{1,0:T(8,128)S(1)}, s32[4,2]{0,1:T(2,128)S(1)}, f32[4,128,128]{2,1,0:T(8,128)S(1)}, s32[]{:T(128)}) %tuple.34), condition=%wide.while_cond, body=%wide.while_body.sunk | while | flops 2 | bytes 131181 | solution.py:57
  452.7 1.3 bitcast_dynamic-update-slice_fusion.2
  454.7 1.3 bitcast_dynamic-update-slice_fusion.2
  456.6 1.3 bitcast_dynamic-update-slice_fusion.2
  458.6 1.3 bitcast_dynamic-update-slice_fusion.2
  460.0 39.6 %custom-call.35 = f32[4,128,128]{1,2,0:T(8,128)S(1)} custom-call(f32[4,128,128]{2,1,0:T(8,128)S(1)} %get-tuple-element.12), custom_call_target="InvertDiagBlocksLowerTriangular" | custom-call | tf_op jit(solution)/shard_map/triangular_solve | solution.py:57
  499.6 1.2 fusion.39
  500.8 1.3 convolution_subtract_fusion.7
  502.4 1.5 convolution_subtract_fusion.4
  507.8 1.3 fusion.5
  509.1 2.5 copy.26
  (67 shorter events, 12.8 us)
Async XLA Ops:
  7.2 357.3 %all-reduce.3.cloned.1.call-start = ((), (), s32[]{:S(2)}) async-start(), calls=%async_computation.1 | async-start | bytes 3145728 | tf_op jit(solution)/shard_map/psum | solution.py:52
  8.0 4.1 copy-start.5
  28.7 6.2 %copy-start.7 = (s32[1024]{0:T(1024)S(1)}, s32[1024]{0:T(1024)}, u32[]{:S(2)}) copy-start(s32[1024]{0:T(1024)} %param.8) | copy-start | bytes 12292
  28.7 6.2 %copy-start.8 = (s32[1024]{0:T(1024)S(1)}, s32[1024]{0:T(1024)}, u32[]{:S(2)}) copy-start(s32[1024]{0:T(1024)} %param.9) | copy-start | bytes 12292
  51.7 48.5 %copy-start.6 = (f32[32,32,1]{1,0,2:T(8,128)S(1)}, f32[32,32,1]{1,0,2:T(8,128)}, u32[]{:S(2)}) copy-start(f32[32,32,1]{1,0,2:T(8,128)} %constant.187) | copy-start | bytes 12292
  103.4 1.1 copy-start.4
  364.5 1.2 slice-start
  364.5 2.5 copy-start.1
  452.0 52.2 %copy-start.2 = (f32[512,768]{0,1:T(8,128)S(1)}, f32[512,768]{0,1:T(8,128)}, u32[]{:S(2)}) copy-start(f32[512,768]{0,1:T(8,128)} %all-reduce.3.cloned.1.call-done) | copy-start | bytes 4718596
  505.4 2.4 copy-start
  507.7 1.4 copy-start.3
Sparse Core Ops, SparseCore 0:
  106.9 257.5 all-reduce.2
where the time goes:
time: 529 us; the launch traced here: 519 us
  waiting for transfers between devices  258 us (49%)
  other arithmetic  125 us (24%)
  blocking collectives  48.5 us (9%)
  matrix products  36.5 us (7%)
  local copies, waits for them, and re-layouts  33.7 us (6%)
  between operations  17.4 us (3%)
    psum x1, waiting for transfers between devices, per_device(): total = lax.psum(gram, ('outer', 'inner'))  258 us
    another operation x14, other arithmetic, per_device(): final_lower = jnp.linalg.cholesky(total[:, :feat_width])  78.6 us
    all_to_all x1, blocking collectives, per_device(): lax.all_to_all(sectioned, 'inner', split_axis=0, concat_axis=0, tiled=True)  48.5 us
    another operation x4, other arithmetic, per_device(): lax.linalg.triangular_solve(final_lower, middle, left_side=True, lower=Tr...  39.7 us
    dot_general x1, matrix products, per_device(): jnp.einsum('ai,ibc->abc', factor, half, precision=lax.Precision.HIGHEST)  16.6 us
  transfers between devices with their start and end apart: 1, of which 1 were waited for; matrix products, arithmetic and copies ran while one was open for 0% of the time, Pallas kernels for 0%

commit v1 on v0

v1 whole, which is shorter than its diff:
```python
import functools
import math

import jax
import jax.numpy as jnp
from jax import lax
from jax.experimental import pallas as pl
from jax.experimental.pallas import tpu as pltpu
from jax.sharding import PartitionSpec as P

F = 512
K = 256
BLOCK = 4096
KEEP = 1024
INNER = 32
NX, NC, NY, NZ = 4, 2, 4, 8
SECTION = KEEP // INNER
TILE = 128
G_BLOCKS = [(i, j) for i in range(4) for j in range(i, 4)]
R_BLOCKS = [(i, j) for i in range(4) for j in range(4, 6)]
G_ROWS = TILE * len(G_BLOCKS)
R_ROWS = TILE * len(R_BLOCKS)
HIGHEST = lax.Precision.HIGHEST
MESH = pl.DeviceIdType.MESH

NN = (((1,), (0,)), ((), ()))
NT = (((1,), (1,)), ((), ()))
TN = (((0,), (0,)), ((), ()))


def dot(a, b, dims=NN, precision=None):
    return lax.dot_general(a, b, dims, precision=precision, preferred_element_type=jnp.float32)


def iota(shape, dim):
    return lax.broadcasted_iota(jnp.int32, shape, dim)


def parity_sign(bits):
    bits = bits ^ (bits >> 8)
    bits = bits ^ (bits >> 4)
    bits = bits ^ (bits >> 2)
    bits = bits ^ (bits >> 1)
    return (1 - 2 * (bits & 1)).astype(jnp.float32)


def position(inner):
    return inner // NZ, lax.rem(inner, NZ)


def order_picks(picks_ref, routes_ref, upper_ref, coded_ref, factors_ref):
    picks = picks_ref[...]
    routes = routes_ref[...]

    @pl.loop(0, KEEP // TILE)
    def _(c):
        at = pl.multiple_of(c * TILE, TILE)
        row = iota((TILE, KEEP), 0) + at
        upper_ref[pl.ds(at, TILE), :] = (row < iota((TILE, KEEP), 1)).astype(jnp.float32).astype(jnp.bfloat16)

    hot = (iota((INNER, KEEP), 0) == routes).astype(jnp.float32)
    before = dot(hot.astype(jnp.bfloat16), upper_ref[...])
    rank = jnp.sum(hot * before, axis=0, keepdims=True)
    place = routes * SECTION + rank.astype(jnp.int32)
    low = iota((TILE, KEEP), 0) & picks
    coded_ref[pl.ds(0, TILE), :] = parity_sign(low).astype(jnp.bfloat16)
    for bit in range(5):
        high = 1 - 2 * ((picks >> (7 + bit)) & 1)
        coded_ref[pl.ds((bit + 1) * TILE, TILE), :] = jnp.broadcast_to(
            high.astype(jnp.float32), (TILE, KEEP)
        ).astype(jnp.bfloat16)

    @pl.loop(0, KEEP // TILE)
    def _(c):
        at = pl.multiple_of(c * TILE, TILE)
        chosen = (iota((TILE, KEEP), 0) + at == place).astype(jnp.float32).astype(jnp.bfloat16)
        factors_ref[pl.ds(at, TILE), :] = dot(chosen, coded_ref[...], NT).astype(jnp.bfloat16)


def fill_signs(signs_ref, flips_ref):
    for q in range(BLOCK // TILE):
        row = (2 * signs_ref[q : q + 1, :] - 1).astype(jnp.float32)
        flips_ref[:, q * TILE : (q + 1) * TILE] = jnp.broadcast_to(row, (16, TILE)).astype(jnp.bfloat16)


def fill_mixer(factors_ref, flips_ref, mixer_ref):
    rows = 64

    @pl.loop(0, KEEP // rows)
    def _(c):
        at = pl.multiple_of(c * rows, rows)
        here = factors_ref[pl.ds(at, rows), 0:TILE]
        gray = 0
        for step in range(BLOCK // TILE):
            if step:
                bit = (step & -step).bit_length() - 1
                gray ^= 1 << bit
                here = here * factors_ref[pl.ds(at, rows), (bit + 1) * TILE : (bit + 2) * TILE]
            flip = flips_ref[:, gray * TILE : (gray + 1) * TILE]
            flip = jnp.concatenate([flip] * (rows // 16), 0)
            mixer_ref[pl.ds(at, rows), gray * TILE : (gray + 1) * TILE] = here * flip


class Part:
    def __init__(self, rows, own, core_in, x_in, y_in, z_in, total, send, recv):
        self.rows = rows
        self.own, self.total = own, total
        self.core_in, self.x_in, self.y_in, self.z_in = core_in, x_in, y_in, z_in
        self.send, self.recv = send, recv
        outer = lax.axis_index("outer")
        self.x, self.core = outer // NC, lax.rem(outer, NC)
        self.y, self.z = position(lax.axis_index("inner"))
        self.half, self.eighth, self.piece = rows // 2, rows // 8, rows // 32
        self.at_half = pl.multiple_of(self.core * self.half, 8)
        self.at_eighth = pl.multiple_of(self.at_half + self.x * self.eighth, 8)
        self.at_piece = pl.multiple_of(self.at_eighth + self.y * self.piece, 8)
        self.copies = {}

    def copy(self, src, dst, slot_out, slot_in, device):
        return pltpu.make_async_remote_copy(
            src_ref=src,
            dst_ref=dst,
            send_sem=self.send.at[slot_out],
            recv_sem=self.recv.at[slot_in],
            device_id=device,
            device_id_type=MESH,
        )

    def start(self, stage):
        copies = []
        if stage == 0:
            other = 1 - self.core
            at = pl.multiple_of(other * self.half, 8)
            copies.append(self.copy(self.own.at[pl.ds(at, self.half)], self.core_in, 0, 0, {"outer": self.x * NC + other}))
        elif stage == 1:
            for d in range(1, NX):
                to = lax.rem(self.x + d, NX)
                at = pl.multiple_of(self.at_half + to * self.eighth, 8)
                copies.append(self.copy(self.own.at[pl.ds(at, self.eighth)], self.x_in.at[d - 1], d, d, {"outer": to * NC + self.core}))
        elif stage == 2:
            for d in range(1, NY):
                to = lax.rem(self.y + d, NY)
                at = pl.multiple_of(self.at_eighth + to * self.piece, 8)
                copies.append(self.copy(self.own.at[pl.ds(at, self.piece)], self.y_in.at[d - 1], 3 + d, 3 + d, {"inner": to * NZ + self.z}))
        elif stage == 3:
            for d in range(1, NZ):
                to = lax.rem(self.z + d, NZ)
                copies.append(
                    self.copy(self.own.at[pl.ds(self.at_piece, self.piece)], self.z_in.at[self.z], 6 + d, 6 + d, {"inner": self.y * NZ + to})
                )
        elif stage == 4:
            for d in range(1, NY):
                to = lax.rem(self.y + d, NY)
                where = self.total.at[pl.ds(self.at_piece, self.piece)]
                copies.append(self.copy(where, where, 13 + d, 13 + d, {"inner": to * NZ + self.z}))
        elif stage == 5:
            for d in range(1, NX):
                to = lax.rem(self.x + d, NX)
                where = self.total.at[pl.ds(self.at_eighth, self.eighth)]
                copies.append(self.copy(where, where, 16 + d, 16 + d, {"outer": to * NC + self.core}))
        else:
            where = self.total.at[pl.ds(self.at_half, self.half)]
            copies.append(self.copy(where, where, 20, 20, {"outer": self.x * NC + 1 - self.core}))
        for c in copies:
            c.start()
        self.copies[stage] = copies

    def finish(self, stage):
        if stage == 3:
            mine = self.own[pl.ds(self.at_piece, self.piece), :]
            self.z_in[self.z] = mine
        for c in self.copies[stage]:
            c.wait()
        if stage == 0:
            at = pl.ds(self.at_half, self.half)
            self.own[at, :] = self.own[at, :] + self.core_in[...]
        elif stage == 1:
            at = pl.ds(self.at_eighth, self.eighth)
            self.own[at, :] = (self.own[at, :] + self.x_in[0]) + (self.x_in[1] + self.x_in[2])
        elif stage == 2:
            at = pl.ds(self.at_piece, self.piece)
            self.own[at, :] = (self.own[at, :] + self.y_in[0]) + (self.y_in[1] + self.y_in[2])
        elif stage == 3:
            t = [self.z_in[i] for i in range(NZ)]
            t = [t[0] + t[1], t[2] + t[3], t[4] + t[5], t[6] + t[7]]
            self.total[pl.ds(self.at_piece, self.piece), :] = (t[0] + t[1]) + (t[2] + t[3])


SEMS = 21


def sketch_kernel(
    features, targets, signs_ref, picks_ref, routes_ref,
    sketch_ref, g_total, r_total,
    feat, targ, upper, coded, factors, flips, mixer,
    out_f, out_k, in_f, in_k,
    g_own, g_core, g_x, g_y, g_z,
    r_own, r_core, r_x, r_y, r_z,
    load_sem, own_sem, send_sem, recv_sem, g_send, g_recv, r_send, r_recv,
):
    outer = lax.axis_index("outer")
    me = lax.axis_index("inner")
    x, core = outer // NC, lax.rem(outer, NC)
    y, _ = position(me)

    loads = [
        pltpu.make_async_copy(features, feat, load_sem.at[0]),
        pltpu.make_async_copy(targets, targ, load_sem.at[1]),
    ]
    for load in loads:
        load.start()

    barrier = pltpu.get_barrier_semaphore()

    @pl.loop(1, INNER)
    def _(d):
        pl.semaphore_signal(barrier, inc=1, device_id={"inner": lax.rem(me + d, INNER)}, device_id_type=MESH)

    pl.semaphore_signal(barrier, inc=1, device_id={"outer": x * NC + 1 - core}, device_id_type=MESH)
    for d in range(1, NX):
        pl.semaphore_signal(barrier, inc=1, device_id={"outer": lax.rem(x + d, NX) * NC + core}, device_id_type=MESH)

    order_picks(picks_ref, routes_ref, upper, coded, factors)
    fill_signs(signs_ref, flips)
    fill_mixer(factors, flips, mixer)
    for load in loads:
        load.wait()
    pl.semaphore_wait(barrier, INNER - 1 + 1 + NX - 1)

    def section(ref, d):
        return ref.at[pl.ds(pl.multiple_of(d * SECTION, SECTION), SECTION)]

    def exchange(kind, out, into, d):
        return pltpu.make_async_remote_copy(
            src_ref=section(out, d),
            dst_ref=section(into, me),
            send_sem=send_sem.at[kind, d],
            recv_sem=recv_sem.at[kind, me],
            device_id={"inner": d},
            device_id_type=MESH,
        )

    span = NZ * SECTION
    for kind, (data, out, into) in enumerate([(feat, out_f, in_f), (targ, out_k, in_k)]):

        @pl.loop(0, NY)
        def _(c):
            row = lax.rem(y + c + 1, NY)
            at = pl.multiple_of(row * span, span)
            kept = dot(mixer[pl.ds(at, span), :], data[...])
            out[pl.ds(at, span), :] = (kept * (1.0 / 64)).astype(jnp.bfloat16)

            @pl.loop(0, NZ)
            def _(i):
                d = row * NZ + lax.rem(me + i + 1, NZ)

                @pl.when(d != me)
                def _():
                    exchange(kind, out, into, d).start()

    own = [
        pltpu.make_async_copy(section(out_f, me), section(in_f, me), own_sem.at[0]),
        pltpu.make_async_copy(section(out_k, me), section(in_k, me), own_sem.at[1]),
    ]
    for copy in own:
        copy.start()

    @pl.loop(0, KEEP // TILE)
    def _(c):
        at = pl.multiple_of(c * TILE, TILE)
        a = iota((TILE, KEEP), 0) + at
        b = iota((TILE, KEEP), 1)
        sign = parity_sign((a // SECTION) & (b // SECTION))
        upper[pl.ds(at, TILE), :] = jnp.where((a ^ b) & (SECTION - 1) == 0, sign, 0.0).astype(jnp.bfloat16)

    def arrive(kind, out, into):
        own[kind].wait()

        @pl.loop(1, INNER)
        def _(i):
            s = lax.rem(me + i, INNER)
            pltpu.make_async_remote_copy(
                src_ref=section(out, s),
                dst_ref=section(into, s),
                send_sem=send_sem.at[kind, s],
                recv_sem=recv_sem.at[kind, s],
                device_id={"inner": s},
                device_id_type=MESH,
            ).wait()

    def mix(into, first, width):
        @pl.loop(0, KEEP // 256)
        def _(c):
            at = pl.multiple_of(c * 256, 256)
            mixed = dot(upper[pl.ds(at, 256), :], into[...])
            sketch_ref[pl.ds(at, 256), first : first + width] = (mixed * (1.0 / math.sqrt(INNER))).astype(jnp.bfloat16)

    g = Part(G_ROWS, g_own, g_core, g_x, g_y, g_z, g_total, g_send, g_recv)
    r = Part(R_ROWS, r_own, r_core, r_x, r_y, r_z, r_total, r_send, r_recv)

    arrive(0, out_f, in_f)
    mix(in_f, 0, F)
    for i in range(4):
        rows = dot(sketch_ref[:, i * TILE : (i + 1) * TILE], sketch_ref[:, i * TILE : F], TN)
        for j in range(i, 4):
            at = G_BLOCKS.index((i, j)) * TILE
            g_own[at : at + TILE, :] = rows[:, (j - i) * TILE : (j - i + 1) * TILE]
    g.start(0)
    g.finish(0)
    g.start(1)
    g.finish(1)
    g.start(2)
    arrive(1, out_k, in_k)
    mix(in_k, F, K)
    for i in range(4):
        rows = dot(sketch_ref[:, i * TILE : (i + 1) * TILE], sketch_ref[:, F:], TN)
        for j in range(4, 6):
            at = R_BLOCKS.index((i, j)) * TILE
            r_own[at : at + TILE, :] = rows[:, (j - 4) * TILE : (j - 3) * TILE]
    r.start(0)
    for stage in range(2, 7):
        g.finish(stage)
        if stage < 6:
            g.start(stage + 1)
        r.finish(stage - 2)
        r.start(stage - 1)
    r.finish(5)
    r.start(6)
    r.finish(6)


def sketch_and_gram(features, targets, signs, picks, routes):
    vmem = pl.BlockSpec(memory_space=pltpu.VMEM)
    hbm = pl.BlockSpec(memory_space=pl.ANY)
    f32, bf16 = jnp.float32, jnp.bfloat16

    def part(rows):
        return [
            pltpu.VMEM((rows, TILE), f32),
            pltpu.VMEM((rows // 2, TILE), f32),
            pltpu.VMEM((NX - 1, rows // 8, TILE), f32),
            pltpu.VMEM((NY - 1, rows // 32, TILE), f32),
            pltpu.VMEM((NZ, rows // 32, TILE), f32),
        ]

    dma = pltpu.SemaphoreType.DMA
    return pl.pallas_call(
        sketch_kernel,
        out_shape=(
            jax.ShapeDtypeStruct((KEEP, F + K), bf16),
            jax.ShapeDtypeStruct((G_ROWS, TILE), f32),
            jax.ShapeDtypeStruct((R_ROWS, TILE), f32),
        ),
        in_specs=[hbm, hbm, vmem, vmem, vmem],
        out_specs=(vmem, vmem, vmem),
        scratch_shapes=[
            pltpu.VMEM((BLOCK, F), bf16),
            pltpu.VMEM((BLOCK, K), bf16),
            pltpu.VMEM((KEEP, KEEP), bf16),
            pltpu.VMEM((6 * TILE, KEEP), bf16),
            pltpu.VMEM((KEEP, 6 * TILE), bf16),
            pltpu.VMEM((16, BLOCK), bf16),
            pltpu.VMEM((KEEP, BLOCK), bf16),
            pltpu.VMEM((KEEP, F), bf16),
            pltpu.VMEM((KEEP, K), bf16),
            pltpu.VMEM((KEEP, F), bf16),
            pltpu.VMEM((KEEP, K), bf16),
        ]
        + part(G_ROWS)
        + part(R_ROWS)
        + [
            dma((2,)), dma((2,)), dma((2, INNER)), dma((2, INNER)),
            dma((SEMS,)), dma((SEMS,)), dma((SEMS,)), dma((SEMS,)),
        ],
        compiler_params=pltpu.CompilerParams(
            collective_id=0, has_side_effects=True, vmem_limit_bytes=56 << 20
        ),
        name="sketch",
    )(features, targets, signs, picks, routes)


def invert(block):
    lane = iota((8, TILE), 1)
    sub = iota((8, TILE), 0)

    def spread(v, j):
        return jnp.broadcast_to(v[:, j : j + 1], (8, TILE))

    def down(v, i):
        return jnp.broadcast_to(v[i : i + 1, :], (8, TILE))

    v = [block[8 * i : 8 * i + 8, :] for i in range(16)]
    for g in range(16):
        base = 8 * g
        now = v[g]
        cols = [spread(now, base + j) for j in range(8)]
        for s in range(8):
            over = 1.0 / down(cols[s], s)
            mult = jnp.where(sub == s, 0.0, cols[s])
            row = jnp.where(lane == base + s, 1.0, down(now, s)) * over
            now = jnp.where(sub == s, row, jnp.where(lane == base + s, 0.0, now) - mult * row)
            for j in range(s + 1, 8):
                pivot = down(cols[j], s) * over
                cols[j] = jnp.where(sub == s, pivot, cols[j] - mult * pivot)
        rows = [down(now, j) for j in range(8)]
        panel = (lane >= base) & (lane < base + 8)
        new = []
        for i in range(16):
            if i == g:
                new.append(now)
                continue
            p = [spread(v[i], base + j) * rows[j] for j in range(8)]
            p = ((p[0] + p[1]) + (p[2] + p[3])) + ((p[4] + p[5]) + (p[6] + p[7]))
            new.append(jnp.where(panel, 0.0, v[i]) - p)
        v = new
    return jnp.concatenate(v, 0)


def solve_kernel(features, g_ref, r_ref, weights_ref, predictions, feat, work, inverse, guess, load_sem, store_sem):
    load = pltpu.make_async_copy(features, feat, load_sem)
    load.start()
    for n, (i, j) in enumerate(G_BLOCKS):
        tile = g_ref[n * TILE : (n + 1) * TILE, :]
        work[i * TILE : (i + 1) * TILE, j * TILE : (j + 1) * TILE] = tile
        if i != j:
            work[j * TILE : (j + 1) * TILE, i * TILE : (i + 1) * TILE] = tile.T
    for n, (i, j) in enumerate(R_BLOCKS):
        work[i * TILE : (i + 1) * TILE, j * TILE : (j + 1) * TILE] = r_ref[n * TILE : (n + 1) * TILE, :]

    @pl.loop(0, F // TILE)
    def _(b):
        at = pl.multiple_of(b * TILE, TILE)
        inverse[...] = invert(work[pl.ds(at, TILE), pl.ds(at, TILE)])
        solved = dot(inverse[...], work[pl.ds(at, TILE), :], precision=HIGHEST)
        row = iota((F, TILE), 0)
        column = jnp.where((row >= at) & (row < at + TILE), 0.0, work[:, pl.ds(at, TILE)])
        work[...] = work[...] - dot(column, solved, precision=HIGHEST)
        work[pl.ds(at, TILE), :] = solved

    weights_ref[...] = work[:, F:]
    narrow = work[:, F:].astype(jnp.bfloat16)
    load.wait()
    chunk = BLOCK // 4
    stores = []
    for c in range(4):
        guess[c * chunk : (c + 1) * chunk, :] = dot(feat[c * chunk : (c + 1) * chunk, :], narrow).astype(jnp.bfloat16)
        store = pltpu.make_async_copy(
            guess.at[pl.ds(c * chunk, chunk)], predictions.at[pl.ds(c * chunk, chunk)], store_sem.at[c]
        )
        store.start()
        stores.append(store)
    for store in stores:
        store.wait()


def solve_and_predict(features, g_total, r_total):
    vmem = pl.BlockSpec(memory_space=pltpu.VMEM)
    hbm = pl.BlockSpec(memory_space=pl.ANY)
    return pl.pallas_call(
        solve_kernel,
        out_shape=(
            jax.ShapeDtypeStruct((F, K), jnp.float32),
            jax.ShapeDtypeStruct((BLOCK, K), jnp.bfloat16),
        ),
        in_specs=[hbm, vmem, vmem],
        out_specs=(vmem, hbm),
        scratch_shapes=[
            pltpu.VMEM((BLOCK, F), jnp.bfloat16),
            pltpu.VMEM((F, F + K), jnp.float32),
            pltpu.VMEM((TILE, TILE), jnp.float32),
            pltpu.VMEM((BLOCK, K), jnp.bfloat16),
            pltpu.SemaphoreType.DMA,
            pltpu.SemaphoreType.DMA((4,)),
        ],
        compiler_params=pltpu.CompilerParams(vmem_limit_bytes=40 << 20),
        name="solve",
    )(features, g_total, r_total)


def per_device(features, targets, signs, picks, routes):
    sketch, g_total, r_total = sketch_and_gram(
        features,
        targets,
        signs.reshape(BLOCK // TILE, TILE),
        picks.reshape(1, KEEP),
        routes.reshape(1, KEEP),
    )
    weights, predictions = solve_and_predict(features, g_total, r_total)
    return (sketch, weights, predictions)


def solution(mesh):
    both = ("outer", "inner")
    in_specs = (P(both, None), P(both, None), P(both), P(both), P(both))
    out_specs = (P(both, None), P(), P(both, None))
    return jax.shard_map(per_device, mesh=mesh, in_specs=in_specs, out_specs=out_specs, check_vma=False)
```

time: 529 us -> 122 us (0.23); the launches traced: 519 us -> 122 us
  waiting for transfers between devices: 258 us -> 0 us
  other arithmetic: 125 us -> 0 us
  Pallas kernels: 0 us -> 118 us
  blocking collectives: 48.5 us -> 0 us
  matrix products: 36.5 us -> 0 us
  local copies, waits for them, and re-layouts: 33.7 us -> 3.27 us
  between operations: 17.4 us -> 0.68 us
    psum x1 -> x0, waiting for transfers between devices: 258 us -> none  [per_device(): total = lax.psum(gram, ('outer', 'inner'))]
    another operation x18 -> x0, other arithmetic: 118 us -> none  [the longest x14 78.6 us: per_device(): final_lower = jnp.linalg.cholesky(total[:, :feat_width])]
    pallas_call x0 -> x2, Pallas kernels: none -> 118 us  [the longest x1 87.9 us: sketch_and_gram(): pl.pallas_call(sketch_kernel, out_shape=(jax.ShapeDtypeStruct((KEEP, F +...]
    all_to_all x1 -> x0, blocking collectives: 48.5 us -> none  [per_device(): lax.all_to_all(sectioned, 'inner', split_axis=0, concat_axis=0, tiled=True)]
    dot_general x5 -> x0, matrix products: 26.5 us -> none  [the longest x1 16.6 us: per_device(): jnp.einsum('ai,ibc->abc', factor, half, precision=lax.Precision.HIGHEST)]
    gather x2 -> x0, local copies, waits for them, and re-layouts: 12.4 us -> none  [the longest x1 8.07 us: per_device(): kept = whole.reshape(block_rows, total_width)[picks].astype(jnp.bfloat16)]
    another operation x20 -> x0, matrix products: 10.1 us -> none  [the longest x7 5.76 us: per_device(): lax.linalg.triangular_solve(final_lower, total[:, feat_width:], left_side...]
    another operation x17 -> x0, local copies, waits for them, and re-layouts: 7.99 us -> none
  transfers between devices with their start and end apart: 1 -> 0, of which waited for: 1 -> 0; matrix products, arithmetic and copies ran while one was open for 0% -> 0% of each run, Pallas kernels for 0% -> 0%
where the time goes in v1:
time: 122 us
  Pallas kernels  118 us (97%)
  local copies, waits for them, and re-layouts  3.27 us (3%)
    pallas_call x1, Pallas kernels, sketch_and_gram(): pl.pallas_call(sketch_kernel, out_shape=(jax.ShapeDtypeStruct((KEEP, F +...  87.9 us
    pallas_call x1, Pallas kernels, solve_and_predict(): pl.pallas_call(solve_kernel, out_shape=(jax.ShapeDtypeStruct((F, K), jnp....  29.9 us
    unnamed x9, local copies, waits for them, and re-layouts  3.27 us

profile of v1, /device:TPU:1, one launch (start us, length us, event | category | flops | bytes accessed | tf_op | source)
XLA Modules:
  0.0 121.8 jit_solution(10127237093017019850)
XLA Ops:
  0.6 0.0 copy-start
  0.6 87.9 %sketch.1 = (bf16[1024,768]{1,0:T(8,128)(2,1)}, f32[1280,128]{1,0:T(8,128)}, f32[1024,128]{1,0:T(8,128)}) custom-call(bf16[4096,512]{1,0:T(8,128)(2,1)} %features.3, bf16[4096,256]{1,0:T(8,128)(2,1)} %targets.1, s32[32,128]{1,0:T(8,128)} %bitcast.3, s32[1,1024]{1,0:T(1,128)} %bitcast.4, s32[1,1024]{1,0:T(1,128)} %bitcast.5), custom_call_target="tpu_custom_call" | custom-call | tf_op jit(solution)/shard_map/sketch/pallas_call | solution.py:347
  88.6 0.0 copy-done
  88.6 0.0 copy-start.1
  88.6 1.1 copy-done.1
  89.7 0.0 copy-start.2
  89.7 1.0 copy-done.2
  90.7 0.0 copy-start.3
  90.7 29.9 %solve.1 = (f32[512,256]{1,0:T(8,128)}, bf16[4096,256]{1,0:T(8,128)(2,1)}) custom-call(bf16[4096,512]{1,0:T(8,128)(2,1)S(1)} %copy-done, f32[1280,128]{1,0:T(8,128)S(1)} %copy-done.1, f32[1024,128]{1,0:T(8,128)S(1)} %copy-done.2), custom_call_target="tpu_custom_call" | custom-call | tf_op jit(solution)/shard_map/solve/pallas_call | solution.py:459
  120.7 0.0 copy-done.3
  120.7 1.1 copy.9
Async XLA Ops:
  0.6 88.0 %copy-start = (bf16[4096,512]{1,0:T(8,128)(2,1)S(1)}, bf16[4096,512]{1,0:T(8,128)(2,1)}, u32[]{:S(2)}) copy-start(bf16[4096,512]{1,0:T(8,128)(2,1)} %features.3) | copy-start | bytes 12582916
  88.6 1.1 copy-start.1
  89.7 1.0 copy-start.2
  90.7 29.9 %copy-start.3 = (bf16[1024,768]{1,0:T(8,128)(2,1)S(1)}, bf16[1024,768]{1,0:T(8,128)(2,1)}, u32[]{:S(2)}) copy-start(bf16[1024,768]{1,0:T(8,128)(2,1)} %get-tuple-element.16) | copy-start | bytes 4718596

commit v2 on v0

v2 whole, which is shorter than its diff:
```python
import functools
import math

import jax
import jax.numpy as jnp
from jax import lax
from jax.experimental import pallas as pl
from jax.experimental.pallas import tpu as pltpu
from jax.sharding import PartitionSpec as P

F = 512
K = 256
BLOCK = 4096
KEEP = 1024
INNER = 32
NX, NC, NY, NZ = 4, 2, 4, 8
SECTION = KEEP // INNER
TILE = 128
G_BLOCKS = [(i, j) for i in range(4) for j in range(i, 4)]
R_BLOCKS = [(i, j) for i in range(4) for j in range(4, 6)]
G_ROWS = TILE * len(G_BLOCKS)
R_ROWS = TILE * len(R_BLOCKS)
HIGHEST = lax.Precision.HIGHEST
MESH = pl.DeviceIdType.MESH

NN = (((1,), (0,)), ((), ()))
NT = (((1,), (1,)), ((), ()))
TN = (((0,), (0,)), ((), ()))


def dot(a, b, dims=NN, precision=None):
    return lax.dot_general(a, b, dims, precision=precision, preferred_element_type=jnp.float32)


def iota(shape, dim):
    return lax.broadcasted_iota(jnp.int32, shape, dim)


def parity_sign(bits):
    bits = bits ^ (bits >> 8)
    bits = bits ^ (bits >> 4)
    bits = bits ^ (bits >> 2)
    bits = bits ^ (bits >> 1)
    return (1 - 2 * (bits & 1)).astype(jnp.float32)


def position(inner):
    return inner // NZ, lax.rem(inner, NZ)


def order_picks(small_ref, upper_ref, coded_ref, factors_ref):
    first = BLOCK // TILE

    def row_of(first):
        return jnp.concatenate([small_ref[first + i : first + i + 1, :] for i in range(KEEP // TILE)], 1)

    picks = row_of(first)
    routes = row_of(first + KEEP // TILE)

    @pl.loop(0, KEEP // TILE)
    def _(c):
        at = pl.multiple_of(c * TILE, TILE)
        row = iota((TILE, KEEP), 0) + at
        upper_ref[pl.ds(at, TILE), :] = (row < iota((TILE, KEEP), 1)).astype(jnp.float32).astype(jnp.bfloat16)

    hot = (iota((INNER, KEEP), 0) == routes).astype(jnp.float32)
    before = dot(hot.astype(jnp.bfloat16), upper_ref[...])
    rank = jnp.sum(hot * before, axis=0, keepdims=True)
    place = routes * SECTION + rank.astype(jnp.int32)
    for n, part in enumerate((picks & (TILE - 1), picks >> 7)):
        coded_ref[n * TILE : (n + 1) * TILE, :] = jnp.broadcast_to(
            part.astype(jnp.float32), (TILE, KEEP)
        ).astype(jnp.bfloat16)

    @pl.loop(0, KEEP // TILE)
    def _(c):
        at = pl.multiple_of(c * TILE, TILE)
        chosen = (iota((TILE, KEEP), 0) + at == place).astype(jnp.float32).astype(jnp.bfloat16)
        found = dot(chosen, coded_ref[...], NT).astype(jnp.int32)
        low = found[:, :TILE] & iota((TILE, TILE), 1)
        factors_ref[pl.ds(at, TILE), :TILE] = parity_sign(low).astype(jnp.bfloat16)
        for bit in range(5):
            high = 1 - 2 * ((found[:, TILE:] >> bit) & 1)
            factors_ref[pl.ds(at, TILE), (bit + 1) * TILE : (bit + 2) * TILE] = high.astype(jnp.float32).astype(jnp.bfloat16)


def fill_signs(signs_ref, flips_ref):
    for q in range(BLOCK // TILE):
        row = (2 * signs_ref[q : q + 1, :] - 1).astype(jnp.float32)
        flips_ref[:, q * TILE : (q + 1) * TILE] = jnp.broadcast_to(row, (16, TILE)).astype(jnp.bfloat16)


def fill_mixer(factors_ref, flips_ref, mixer_ref):
    rows = 64

    @pl.loop(0, KEEP // rows)
    def _(c):
        at = pl.multiple_of(c * rows, rows)
        here = factors_ref[pl.ds(at, rows), 0:TILE]
        gray = 0
        for step in range(BLOCK // TILE):
            if step:
                bit = (step & -step).bit_length() - 1
                gray ^= 1 << bit
                here = here * factors_ref[pl.ds(at, rows), (bit + 1) * TILE : (bit + 2) * TILE]
            flip = flips_ref[:, gray * TILE : (gray + 1) * TILE]
            flip = jnp.concatenate([flip] * (rows // 16), 0)
            mixer_ref[pl.ds(at, rows), gray * TILE : (gray + 1) * TILE] = here * flip


SIZES = {"core": NC, "x": NX, "y": NY, "z": NZ}


def flow_scratch(rows, stages):
    shapes, count = [], 0
    for kind, axis in stages:
        n = SIZES[axis]
        count += n - 1
        if kind == "scatter":
            rows //= n
            shapes.append((n - 1, rows, TILE))
        elif kind == "exchange":
            shapes.append((n, rows, TILE))
        else:
            rows *= n
    return shapes, count


class Flow:
    def __init__(self, own, total, first, rows, stages, landing, send, recv):
        self.own, self.total, self.at, self.rows = own, total, first, rows
        self.stages, self.landing, self.send, self.recv = list(stages), list(landing), send, recv
        self.slot = 0
        self.exchanges_left = sum(kind == "exchange" for kind, _ in stages)
        outer = lax.axis_index("outer")
        inner = lax.axis_index("inner")
        self.place = {"x": outer // NC, "core": lax.rem(outer, NC), "y": inner // NZ, "z": lax.rem(inner, NZ)}

    def device(self, axis, to):
        p = self.place
        if axis == "x":
            return {"outer": to * NC + p["core"]}
        if axis == "core":
            return {"outer": p["x"] * NC + to}
        if axis == "y":
            return {"inner": to * NZ + p["z"]}
        return {"inner": p["y"] * NZ + to}

    def start(self):
        kind, axis = self.stages.pop(0)
        n, me = SIZES[axis], self.place[axis]
        buffer = None if kind == "gather" else self.landing.pop(0)
        copies = []
        for d in range(1, n):
            to = lax.rem(me + d, n)
            if kind == "scatter":
                piece = self.rows // n
                src = self.own.at[pl.ds(pl.multiple_of(self.at + to * piece, 8), piece)]
                dst = buffer.at[d - 1]
            elif kind == "exchange":
                src = self.own.at[pl.ds(pl.multiple_of(self.at, 8), self.rows)]
                dst = buffer.at[me]
            else:
                src = dst = self.total.at[pl.ds(pl.multiple_of(self.at, 8), self.rows)]
            copies.append(
                pltpu.make_async_remote_copy(
                    src_ref=src,
                    dst_ref=dst,
                    send_sem=self.send.at[self.slot],
                    recv_sem=self.recv.at[self.slot],
                    device_id=self.device(axis, to),
                    device_id_type=MESH,
                )
            )
            self.slot += 1
        for copy in copies:
            copy.start()
        self.flight = kind, axis, buffer, copies

    def finish(self):
        kind, axis, buffer, copies = self.flight
        n, me = SIZES[axis], self.place[axis]
        if kind == "exchange":
            buffer[me] = self.own[pl.ds(pl.multiple_of(self.at, 8), self.rows), :]
        for copy in copies:
            copy.wait()
        if kind == "scatter":
            self.rows //= n
            self.at = self.at + me * self.rows
            where = pl.ds(pl.multiple_of(self.at, 8), self.rows)
            terms = [self.own[where, :]] + [buffer[i] for i in range(n - 1)]
        elif kind == "exchange":
            where = pl.ds(pl.multiple_of(self.at, 8), self.rows)
            terms = [buffer[i] for i in range(n)]
        else:
            self.at = self.at - me * self.rows
            self.rows *= n
            return
        while len(terms) > 1:
            terms = [terms[i] + terms[i + 1] for i in range(0, len(terms), 2)]
        self.exchanges_left -= kind == "exchange"
        into = self.own if self.exchanges_left else self.total
        into[where, :] = terms[0]

    def step(self):
        if getattr(self, "flight", None):
            self.finish()
            self.flight = None
        if self.stages:
            self.start()

    def done(self):
        return not self.stages and self.flight is None


CORE = [("scatter", "core")]
FLOW_X = [("scatter", "x"), ("scatter", "y"), ("exchange", "z"), ("gather", "y"), ("gather", "x")]
FLOW_Y = [("scatter", "y"), ("scatter", "x"), ("exchange", "z"), ("gather", "x"), ("gather", "y")]
FLOW_Z = [("scatter", "z"), ("exchange", "x"), ("exchange", "y"), ("gather", "z")]
G_FLOWS = [(256, FLOW_X), (256, FLOW_Y), (128, FLOW_Z)]
R_FLOWS = [(256, FLOW_X), (256, FLOW_Y)]


class Sum:
    def __init__(self, own, total, rows, flows, landing, send, recv):
        self.core = Flow(own, total, 0, rows, CORE + [("gather", "core")], landing[:1], send, recv)
        self.core.exchanges_left = 1
        self.flows, self.args = None, (own, total, rows, flows, landing[1:], send, recv)
        self.phase = 0

    def step(self):
        if self.phase == 0:
            self.core.step()
        elif self.phase == 1:
            self.core.finish()
            self.core.flight = None
            own, total, rows, flows, landing, send, recv = self.args
            at, base, self.flows = self.core.at, 2, []
            for size, stages in flows:
                shapes, count = flow_scratch(size, stages)
                used = [landing.pop(0) for _ in shapes]
                flow = Flow(own, total, at, size, stages, used, send, recv)
                flow.slot = base
                base += count
                at = at + size
                flow.step()
                self.flows.append(flow)
        elif not all(flow.done() for flow in self.flows):
            for flow in self.flows:
                if not flow.done():
                    flow.step()
            if all(flow.done() for flow in self.flows):
                self.core.step()
        else:
            self.core.step()
            self.finished = True
        self.phase += 1

    finished = False


def sum_scratch(rows, flows):
    shapes, count = flow_scratch(rows, CORE)
    count += 1
    for size, stages in flows:
        more, n = flow_scratch(size, stages)
        shapes, count = shapes + more, count + n
    return shapes, count


def invert(block):
    lane = iota((8, TILE), 1)
    sub = iota((8, TILE), 0)

    def spread(v, j):
        return jnp.broadcast_to(v[:, j : j + 1], (8, TILE))

    def down(v, i):
        return jnp.broadcast_to(v[i : i + 1, :], (8, TILE))

    v = [block[8 * i : 8 * i + 8, :] for i in range(16)]
    for g in range(16):
        base = 8 * g
        now = v[g]
        cols = [spread(now, base + j) for j in range(8)]
        for s in range(8):
            over = 1.0 / down(cols[s], s)
            mult = jnp.where(sub == s, 0.0, cols[s])
            row = jnp.where(lane == base + s, 1.0, down(now, s)) * over
            now = jnp.where(sub == s, row, jnp.where(lane == base + s, 0.0, now) - mult * row)
            for j in range(s + 1, 8):
                pivot = down(cols[j], s) * over
                cols[j] = jnp.where(sub == s, pivot, cols[j] - mult * pivot)
        rows = [down(now, j) for j in range(8)]
        panel = (lane >= base) & (lane < base + 8)
        new = []
        for i in range(16):
            if i == g:
                new.append(now)
                continue
            p = [spread(v[i], base + j) * rows[j] for j in range(8)]
            p = ((p[0] + p[1]) + (p[2] + p[3])) + ((p[4] + p[5]) + (p[6] + p[7]))
            new.append(jnp.where(panel, 0.0, v[i]) - p)
        v = new
    return jnp.concatenate(v, 0)


def fill_kron(kron):
    @pl.loop(0, KEEP // TILE)
    def _(c):
        at = pl.multiple_of(c * TILE, TILE)
        a = iota((TILE, KEEP), 0) + at
        b = iota((TILE, KEEP), 1)
        sign = parity_sign((a // SECTION) & (b // SECTION))
        kron[pl.ds(at, TILE), :] = jnp.where((a ^ b) & (SECTION - 1) == 0, sign, 0.0).astype(jnp.bfloat16)


EARLY = {(0, 0), (0, 1)}


def sketch_kernel(
    features, targets, small_ref,
    sketch_hbm, weights_ref,
    feat, targ, upper, coded, factors, flips, mixer,
    out_f, out_k, in_f, in_k, sketch, work, inverse, g_own, g_total, r_own, r_total,
    load_sem, own_sem, store_sem, send_sem, recv_sem, g_send, g_recv, r_send, r_recv, *landing
):
    outer = lax.axis_index("outer")
    me = lax.axis_index("inner")
    x, core = outer // NC, lax.rem(outer, NC)
    y, _ = position(me)

    loads = [
        pltpu.make_async_copy(features, feat, load_sem.at[0]),
        pltpu.make_async_copy(targets, targ, load_sem.at[1]),
    ]
    for load in loads:
        load.start()

    barrier = pltpu.get_barrier_semaphore()

    @pl.loop(1, INNER)
    def _(d):
        pl.semaphore_signal(barrier, inc=1, device_id={"inner": lax.rem(me + d, INNER)}, device_id_type=MESH)

    pl.semaphore_signal(barrier, inc=1, device_id={"outer": x * NC + 1 - core}, device_id_type=MESH)
    for d in range(1, NX):
        pl.semaphore_signal(barrier, inc=1, device_id={"outer": lax.rem(x + d, NX) * NC + core}, device_id_type=MESH)

    order_picks(small_ref, upper, coded, factors)
    fill_signs(small_ref, flips)
    fill_mixer(factors, flips, mixer)
    pl.semaphore_wait(barrier, INNER - 1 + 1 + NX - 1)

    def section(ref, d):
        return ref.at[pl.ds(pl.multiple_of(d * SECTION, SECTION), SECTION)]

    pairs = [(feat, out_f, in_f), (targ, out_k, in_k)]

    def exchange(kind, to, source):
        _, out, into = pairs[kind]
        return pltpu.make_async_remote_copy(
            src_ref=section(out, to),
            dst_ref=section(into, source),
            send_sem=send_sem.at[kind, to],
            recv_sem=recv_sem.at[kind, source],
            device_id={"inner": to},
            device_id_type=MESH,
        )

    span = NZ * SECTION

    def keep(kind, c):
        data, out, _ = pairs[kind]
        at = pl.multiple_of(lax.rem(y + c + 1, NY) * span, span)
        kept = dot(mixer[pl.ds(at, span), :], data[...])
        out[pl.ds(at, span), :] = (kept * (1.0 / 64)).astype(jnp.bfloat16)

    def send(kind, c):
        row = lax.rem(y + c + 1, NY)

        @pl.loop(0, NZ)
        def _(i):
            to = row * NZ + lax.rem(me + i + 1, NZ)

            @pl.when(to != me)
            def _():
                exchange(kind, to, me).start()

    def make(kind):
        loads[kind].wait()
        early = [c for c in range(NY) if (kind, c) in EARLY]
        if early:
            assert early == list(range(len(early)))

            @pl.loop(0, len(early))
            def _(c):
                keep(kind, c)
                send(kind, c)

        @pl.loop(len(early), NY)
        def _(c):
            keep(kind, c)

    def send_rest(kind):
        late = [c for c in range(NY) if (kind, c) not in EARLY]

        @pl.loop(late[0], NY)
        def _(c):
            send(kind, c)

    def arrive(kind):
        own[kind].wait()

        @pl.loop(1, INNER)
        def _(i):
            s = lax.rem(me + i, INNER)
            exchange(kind, s, s).wait()

    def mix(kind):
        first, width = ((0, F), (F, K))[kind]
        into = pairs[kind][2]

        @pl.loop(0, KEEP // 256)
        def _(c):
            at = pl.multiple_of(c * 256, 256)
            mixed = dot(upper[pl.ds(at, 256), :], into[...])
            sketch[pl.ds(at, 256), first : first + width] = (mixed * (1.0 / math.sqrt(INNER))).astype(jnp.bfloat16)

    def eliminate(b, columns):
        at = b * TILE
        pivot = dot(inverse[b], work[at : at + TILE, columns], precision=HIGHEST)
        for first, last in ((0, at), (at + TILE, F)):
            if first < last:
                work[first:last, columns] = work[first:last, columns] - dot(
                    work[first:last, at : at + TILE], pivot, precision=HIGHEST
                )
        work[at : at + TILE, columns] = pivot

    count = len(landing) - len(sum_scratch(R_ROWS, R_FLOWS)[0])
    g = Sum(g_own, g_total, G_ROWS, G_FLOWS, list(landing[:count]), g_send, g_recv)
    r = Sum(r_own, r_total, R_ROWS, R_FLOWS, list(landing[count:]), r_send, r_recv)

    make(0)
    for i in (0, 2):
        rows = dot(out_f[:, i * TILE : (i + 2) * TILE], out_f[:, i * TILE :], TN)
        for n, (p, q) in enumerate(G_BLOCKS):
            if p in (i, i + 1):
                g_own[n * TILE : (n + 1) * TILE, :] = rows[(p - i) * TILE : (p - i + 1) * TILE, (q - i) * TILE : (q - i + 1) * TILE]
    g.step()
    make(1)
    own = [
        pltpu.make_async_copy(section(out_f, me), section(in_f, me), own_sem.at[0]),
        pltpu.make_async_copy(section(out_k, me), section(in_k, me), own_sem.at[1]),
    ]
    for copy in own:
        copy.start()
    g.step()
    for i in (0, 2):
        rows = dot(out_f[:, i * TILE : (i + 2) * TILE], out_k[...], TN)
        for n, (p, q) in enumerate(R_BLOCKS):
            if p in (i, i + 1):
                r_own[n * TILE : (n + 1) * TILE, :] = rows[(p - i) * TILE : (p - i + 1) * TILE, (q - 4) * TILE : (q - 3) * TILE]
    fill_kron(upper)
    g.step()
    r.step()
    while not g.finished:
        g.step()
        r.step()
    send_rest(0)
    send_rest(1)

    for n, (i, j) in enumerate(G_BLOCKS):
        tile = g_total[n * TILE : (n + 1) * TILE, :]
        work[i * TILE : (i + 1) * TILE, j * TILE : (j + 1) * TILE] = tile
        if i != j:
            work[j * TILE : (j + 1) * TILE, i * TILE : (i + 1) * TILE] = tile.T
    targets_at = slice(F, F + K)
    for b in range(F // TILE):
        at = b * TILE
        inverse[b] = invert(work[at : at + TILE, at : at + TILE])
        if b < 3:
            eliminate(b, slice(at + TILE, F))
        if not r.finished:
            r.step()
        if b == 1:
            while not r.finished:
                r.step()
            for n, (i, j) in enumerate(R_BLOCKS):
                work[i * TILE : (i + 1) * TILE, j * TILE : (j + 1) * TILE] = r_total[n * TILE : (n + 1) * TILE, :]
            eliminate(0, targets_at)
        if b:
            eliminate(b, targets_at)
        if b == 2:
            arrive(0)
            mix(0)
            arrive(1)
            mix(1)
            store = pltpu.make_async_copy(sketch, sketch_hbm, store_sem)
            store.start()
    weights_ref[...] = work[:, targets_at]
    store.wait()


def sketch_and_weights(features, targets, small):
    vmem = pl.BlockSpec(memory_space=pltpu.VMEM)
    hbm = pl.BlockSpec(memory_space=pl.ANY)
    f32, bf16 = jnp.float32, jnp.bfloat16
    dma = pltpu.SemaphoreType.DMA
    g_shapes, g_count = sum_scratch(G_ROWS, G_FLOWS)
    r_shapes, r_count = sum_scratch(R_ROWS, R_FLOWS)
    return pl.pallas_call(
        sketch_kernel,
        out_shape=(
            jax.ShapeDtypeStruct((KEEP, F + K), bf16),
            jax.ShapeDtypeStruct((F, K), f32),
        ),
        in_specs=[hbm, hbm, vmem],
        out_specs=(hbm, vmem),
        scratch_shapes=[
            pltpu.VMEM((BLOCK, F), bf16),
            pltpu.VMEM((BLOCK, K), bf16),
            pltpu.VMEM((KEEP, KEEP), bf16),
            pltpu.VMEM((2 * TILE, KEEP), bf16),
            pltpu.VMEM((KEEP, 6 * TILE), bf16),
            pltpu.VMEM((16, BLOCK), bf16),
            pltpu.VMEM((KEEP, BLOCK), bf16),
            pltpu.VMEM((KEEP, F), bf16),
            pltpu.VMEM((KEEP, K), bf16),
            pltpu.VMEM((KEEP, F), bf16),
            pltpu.VMEM((KEEP, K), bf16),
            pltpu.VMEM((KEEP, F + K), bf16),
            pltpu.VMEM((F, F + K), f32),
            pltpu.VMEM((F // TILE, TILE, TILE), f32),
            pltpu.VMEM((G_ROWS, TILE), f32),
            pltpu.VMEM((G_ROWS, TILE), f32),
            pltpu.VMEM((R_ROWS, TILE), f32),
            pltpu.VMEM((R_ROWS, TILE), f32),
            dma((2,)), dma((2,)), dma, dma((2, INNER)), dma((2, INNER)),
            dma((g_count,)), dma((g_count,)), dma((r_count,)), dma((r_count,)),
        ]
        + [pltpu.VMEM(shape, f32) for shape in g_shapes + r_shapes],
        compiler_params=pltpu.CompilerParams(
            collective_id=0, has_side_effects=True, vmem_limit_bytes=51 << 20
        ),
        name="sketch",
    )(features, targets, small)


def predict_kernel(feat, weights_in, sketch_in, sketch_ref, weights_ref, predictions, guess, copy_sem, store_sem):
    copy = pltpu.make_async_copy(sketch_in, sketch_ref, copy_sem)
    copy.start()
    weights_ref[...] = weights_in[...]
    narrow = weights_in[...].astype(jnp.bfloat16)
    chunk = BLOCK // 8
    stores = []
    for c in range(8):
        rows = slice(c * chunk, (c + 1) * chunk)
        guess[rows, :] = dot(feat[rows, :], narrow).astype(jnp.bfloat16)
        where = pl.ds(c * chunk, chunk)
        store = pltpu.make_async_copy(guess.at[where], predictions.at[where], store_sem.at[c])
        store.start()
        stores.append(store)
    for store in stores:
        store.wait()
    copy.wait()


def predict(features, weights, sketch):
    vmem = pl.BlockSpec(memory_space=pltpu.VMEM)
    hbm = pl.BlockSpec(memory_space=pl.ANY)
    return pl.pallas_call(
        predict_kernel,
        out_shape=(
            jax.ShapeDtypeStruct((KEEP, F + K), jnp.bfloat16),
            jax.ShapeDtypeStruct((F, K), jnp.float32),
            jax.ShapeDtypeStruct((BLOCK, K), jnp.bfloat16),
        ),
        in_specs=[vmem, vmem, hbm],
        out_specs=(hbm, vmem, hbm),
        scratch_shapes=[
            pltpu.VMEM((BLOCK, K), jnp.bfloat16),
            pltpu.SemaphoreType.DMA,
            pltpu.SemaphoreType.DMA((8,)),
        ],
        compiler_params=pltpu.CompilerParams(vmem_limit_bytes=12 << 20),
        name="predict",
    )(features, weights, sketch)


def per_device(features, targets, signs, picks, routes):
    sketch, weights = sketch_and_weights(
        features,
        targets,
        jnp.concatenate([signs, picks, routes]).reshape((BLOCK + 2 * KEEP) // TILE, TILE),
    )
    return predict(features, weights, sketch)


def solution(mesh):
    both = ("outer", "inner")
    in_specs = (P(both, None), P(both, None), P(both), P(both), P(both))
    out_specs = (P(both, None), P(), P(both, None))
    return jax.shard_map(per_device, mesh=mesh, in_specs=in_specs, out_specs=out_specs, check_vma=False)
```

time: 529 us -> 86.8 us (0.16)
  the two profiles are of different devices: /device:TPU:1 before, /device:TPU:26 now
where the time goes in v2:
time: 86.8 us; the launch traced here: 86.6 us
  Pallas kernels  85.1 us (98%)
    pallas_call x1, Pallas kernels, sketch_and_weights(): pl.pallas_call(sketch_kernel, out_shape=(jax.ShapeDtypeStruct((KEEP, F +...  81.8 us
    pallas_call x1, Pallas kernels, predict(): pl.pallas_call(predict_kernel, out_shape=(jax.ShapeDtypeStruct((KEEP, F +...  3.27 us

profile of v2, /device:TPU:26, one launch (start us, length us, event | category | flops | bytes accessed | tf_op | source)
XLA Modules:
  0.0 86.6 jit_solution(7105570111867112224)
XLA Ops:
  0.6 0.8 add_bitcast_fusion.small_ref
  1.4 0.0 copy-start
  1.4 81.8 %sketch.1 = (bf16[1024,768]{1,0:T(8,128)(2,1)S(1)}, f32[512,256]{1,0:T(8,128)S(1)}) custom-call(bf16[4096,512]{1,0:T(8,128)(2,1)} %feat.1, bf16[4096,256]{1,0:T(8,128)(2,1)} %targets.1, s32[48,128]{1,0:T(8,128)S(1)} %add_bitcast_fusion.small_ref), custom_call_target="tpu_custom_call" | custom-call | tf_op jit(solution)/shard_map/sketch/pallas_call | solution.py:512
  83.2 0.0 copy-done
  83.2 3.3 %predict.1 = (bf16[1024,768]{1,0:T(8,128)(2,1)}, f32[512,256]{1,0:T(8,128)}, bf16[4096,256]{1,0:T(8,128)(2,1)}) custom-call(bf16[4096,512]{1,0:T(8,128)(2,1)S(1)} %copy-done, f32[512,256]{1,0:T(8,128)S(1)} %get-tuple-element.5.weights_in, bf16[1024,768]{1,0:T(8,128)(2,1)S(1)} %get-tuple-element.6.sketch_in), custom_call_target="tpu_custom_call" | custom-call | tf_op jit(solution)/shard_map/predict/pallas_call | solution.py:572
Async XLA Ops:
  1.4 81.8 %copy-start = (bf16[4096,512]{1,0:T(8,128)(2,1)S(1)}, bf16[4096,512]{1,0:T(8,128)(2,1)}, u32[]{:S(2)}) copy-start(bf16[4096,512]{1,0:T(8,128)(2,1)} %feat.1) | copy-start | bytes 12582916

commit v3 on v2

--- a/solution.py
+++ b/solution.py
@@ -37,7 +37,6 @@
 
 
 def parity_sign(bits):
-    bits = bits ^ (bits >> 8)
     bits = bits ^ (bits >> 4)
     bits = bits ^ (bits >> 2)
     bits = bits ^ (bits >> 1)
@@ -57,11 +56,11 @@
     picks = row_of(first)
     routes = row_of(first + KEEP // TILE)
 
-    @pl.loop(0, KEEP // TILE)
-    def _(c):
-        at = pl.multiple_of(c * TILE, TILE)
-        row = iota((TILE, KEEP), 0) + at
-        upper_ref[pl.ds(at, TILE), :] = (row < iota((TILE, KEEP), 1)).astype(jnp.float32).astype(jnp.bfloat16)
+    above = (iota((TILE, TILE), 0) < iota((TILE, TILE), 1)).astype(jnp.float32).astype(jnp.bfloat16)
+    for q in range(KEEP // TILE):
+        for p in range(KEEP // TILE):
+            tile = above if p == q else jnp.full((TILE, TILE), float(p > q), jnp.bfloat16)
+            upper_ref[q * TILE : (q + 1) * TILE, p * TILE : (p + 1) * TILE] = tile
 
     hot = (iota((INNER, KEEP), 0) == routes).astype(jnp.float32)
     before = dot(hot.astype(jnp.bfloat16), upper_ref[...])
@@ -72,16 +71,18 @@
             part.astype(jnp.float32), (TILE, KEEP)
         ).astype(jnp.bfloat16)
 
-    @pl.loop(0, KEEP // TILE)
+    rows = 2 * TILE
+
+    @pl.loop(0, KEEP // rows)
     def _(c):
-        at = pl.multiple_of(c * TILE, TILE)
-        chosen = (iota((TILE, KEEP), 0) + at == place).astype(jnp.float32).astype(jnp.bfloat16)
+        at = pl.multiple_of(c * rows, rows)
+        chosen = (iota((rows, KEEP), 0) + at == place).astype(jnp.float32).astype(jnp.bfloat16)
         found = dot(chosen, coded_ref[...], NT).astype(jnp.int32)
-        low = found[:, :TILE] & iota((TILE, TILE), 1)
-        factors_ref[pl.ds(at, TILE), :TILE] = parity_sign(low).astype(jnp.bfloat16)
+        low = found[:, :TILE] & iota((rows, TILE), 1)
+        factors_ref[pl.ds(at, rows), :TILE] = parity_sign(low).astype(jnp.bfloat16)
         for bit in range(5):
             high = 1 - 2 * ((found[:, TILE:] >> bit) & 1)
-            factors_ref[pl.ds(at, TILE), (bit + 1) * TILE : (bit + 2) * TILE] = high.astype(jnp.float32).astype(jnp.bfloat16)
+            factors_ref[pl.ds(at, rows), (bit + 1) * TILE : (bit + 2) * TILE] = high.astype(jnp.float32).astype(jnp.bfloat16)
 
 
 def fill_signs(signs_ref, flips_ref):
@@ -216,8 +217,7 @@
 CORE = [("scatter", "core")]
 FLOW_X = [("scatter", "x"), ("scatter", "y"), ("exchange", "z"), ("gather", "y"), ("gather", "x")]
 FLOW_Y = [("scatter", "y"), ("scatter", "x"), ("exchange", "z"), ("gather", "x"), ("gather", "y")]
-FLOW_Z = [("scatter", "z"), ("exchange", "x"), ("exchange", "y"), ("gather", "z")]
-G_FLOWS = [(256, FLOW_X), (256, FLOW_Y), (128, FLOW_Z)]
+G_FLOWS = [(384, FLOW_X), (256, FLOW_Y)]
 R_FLOWS = [(256, FLOW_X), (256, FLOW_Y)]
 
 
@@ -306,13 +306,13 @@
 
 
 def fill_kron(kron):
-    @pl.loop(0, KEEP // TILE)
-    def _(c):
-        at = pl.multiple_of(c * TILE, TILE)
-        a = iota((TILE, KEEP), 0) + at
-        b = iota((TILE, KEEP), 1)
-        sign = parity_sign((a // SECTION) & (b // SECTION))
-        kron[pl.ds(at, TILE), :] = jnp.where((a ^ b) & (SECTION - 1) == 0, sign, 0.0).astype(jnp.bfloat16)
+    a, b = iota((TILE, TILE), 0), iota((TILE, TILE), 1)
+    sign = parity_sign((a // SECTION) & (b // SECTION))
+    tile = jnp.where((a ^ b) & (SECTION - 1) == 0, sign, 0.0)
+    tiles = [tile.astype(jnp.bfloat16), (-tile).astype(jnp.bfloat16)]
+    for q in range(KEEP // TILE):
+        for p in range(KEEP // TILE):
+            kron[q * TILE : (q + 1) * TILE, p * TILE : (p + 1) * TILE] = tiles[(q & p).bit_count() & 1]
 
 
 EARLY = {(0, 0), (0, 1)}
@@ -462,13 +462,20 @@
             if p in (i, i + 1):
                 r_own[n * TILE : (n + 1) * TILE, :] = rows[(p - i) * TILE : (p - i + 1) * TILE, (q - 4) * TILE : (q - 3) * TILE]
     fill_kron(upper)
-    g.step()
     r.step()
-    while not g.finished:
-        g.step()
-        r.step()
+    g.step()
+    r.step()
+    g.step()
+    r.step()
+    g.step()
+    r.step()
     send_rest(0)
     send_rest(1)
+    g.step()
+    g.step()
+    r.step()
+    g.step()
+    assert g.finished
 
     for n, (i, j) in enumerate(G_BLOCKS):
         tile = g_total[n * TILE : (n + 1) * TILE, :]
@@ -481,11 +488,12 @@
         inverse[b] = invert(work[at : at + TILE, at : at + TILE])
         if b < 3:
             eliminate(b, slice(at + TILE, F))
-        if not r.finished:
+        if b == 0:
             r.step()
         if b == 1:
-            while not r.finished:
-                r.step()
+            r.step()
+            r.step()
+            assert r.finished
             for n, (i, j) in enumerate(R_BLOCKS):
                 work[i * TILE : (i + 1) * TILE, j * TILE : (j + 1) * TILE] = r_total[n * TILE : (n + 1) * TILE, :]
             eliminate(0, targets_at)
@@ -494,11 +502,11 @@
         if b == 2:
             arrive(0)
             mix(0)
-            arrive(1)
-            mix(1)
-            store = pltpu.make_async_copy(sketch, sketch_hbm, store_sem)
-            store.start()
     weights_ref[...] = work[:, targets_at]
+    arrive(1)
+    mix(1)
+    store = pltpu.make_async_copy(sketch, sketch_hbm, store_sem)
+    store.start()
     store.wait()
 
 

time: 86.8 us -> 82.6 us (0.952)
  the two profiles are of different devices: /device:TPU:26 before, /device:TPU:1 now
where the time goes in v3:
time: 82.6 us; the launch traced here: 82.4 us
  Pallas kernels  80.8 us (98%)
  between operations  0.83 us (1%)
    pallas_call x1, Pallas kernels, sketch_and_weights(): pl.pallas_call(sketch_kernel, out_shape=(jax.ShapeDtypeStruct((KEEP, F +...  77.5 us
    pallas_call x1, Pallas kernels, predict(): pl.pallas_call(predict_kernel, out_shape=(jax.ShapeDtypeStruct((KEEP, F +...  3.27 us

profile of v3, /device:TPU:1, one launch (start us, length us, event | category | flops | bytes accessed | tf_op | source)
XLA Modules:
  0.0 82.4 jit_solution(2333986595701405364)
XLA Ops:
  0.6 0.8 add_bitcast_fusion.small_ref
  1.4 0.0 copy-start
  1.4 77.5 %sketch.1 = (bf16[1024,768]{1,0:T(8,128)(2,1)S(1)}, f32[512,256]{1,0:T(8,128)S(1)}) custom-call(bf16[4096,512]{1,0:T(8,128)(2,1)} %feat.1, bf16[4096,256]{1,0:T(8,128)(2,1)} %targets.1, s32[48,128]{1,0:T(8,128)S(1)} %add_bitcast_fusion.small_ref), custom_call_target="tpu_custom_call" | custom-call | tf_op jit(solution)/shard_map/sketch/pallas_call | solution.py:520
  78.9 0.0 copy-done
  78.9 3.3 %predict.1 = (bf16[1024,768]{1,0:T(8,128)(2,1)}, f32[512,256]{1,0:T(8,128)}, bf16[4096,256]{1,0:T(8,128)(2,1)}) custom-call(bf16[4096,512]{1,0:T(8,128)(2,1)S(1)} %copy-done, f32[512,256]{1,0:T(8,128)S(1)} %get-tuple-element.5.weights_in, bf16[1024,768]{1,0:T(8,128)(2,1)S(1)} %get-tuple-element.6.sketch_in), custom_call_target="tpu_custom_call" | custom-call | tf_op jit(solution)/shard_map/predict/pallas_call | solution.py:580
Async XLA Ops:
  1.4 77.6 %copy-start = (bf16[4096,512]{1,0:T(8,128)(2,1)S(1)}, bf16[4096,512]{1,0:T(8,128)(2,1)}, u32[]{:S(2)}) copy-start(bf16[4096,512]{1,0:T(8,128)(2,1)} %feat.1) | copy-start | bytes 12582916

commit v4 on v3

--- a/solution.py
+++ b/solution.py
@@ -109,7 +109,7 @@
             mixer_ref[pl.ds(at, rows), gray * TILE : (gray + 1) * TILE] = here * flip
 
 
-SIZES = {"core": NC, "x": NX, "y": NY, "z": NZ}
+SIZES = {"core": NC, "plane": NX * NY, "z": NZ}
 
 
 def flow_scratch(rows, stages):
@@ -135,17 +135,15 @@
         self.exchanges_left = sum(kind == "exchange" for kind, _ in stages)
         outer = lax.axis_index("outer")
         inner = lax.axis_index("inner")
-        self.place = {"x": outer // NC, "core": lax.rem(outer, NC), "y": inner // NZ, "z": lax.rem(inner, NZ)}
+        self.x, self.y = outer // NC, inner // NZ
+        self.place = {"core": lax.rem(outer, NC), "plane": self.x * NY + self.y, "z": lax.rem(inner, NZ)}
 
     def device(self, axis, to):
-        p = self.place
-        if axis == "x":
-            return {"outer": to * NC + p["core"]}
         if axis == "core":
-            return {"outer": p["x"] * NC + to}
-        if axis == "y":
-            return {"inner": to * NZ + p["z"]}
-        return {"inner": p["y"] * NZ + to}
+            return {"outer": self.x * NC + to}
+        if axis == "plane":
+            return {"outer": (to // NY) * NC + self.place["core"], "inner": lax.rem(to, NY) * NZ + self.place["z"]}
+        return {"inner": self.y * NZ + to}
 
     def start(self):
         kind, axis = self.stages.pop(0)
@@ -215,10 +213,9 @@
 
 
 CORE = [("scatter", "core")]
-FLOW_X = [("scatter", "x"), ("scatter", "y"), ("exchange", "z"), ("gather", "y"), ("gather", "x")]
-FLOW_Y = [("scatter", "y"), ("scatter", "x"), ("exchange", "z"), ("gather", "x"), ("gather", "y")]
-G_FLOWS = [(384, FLOW_X), (256, FLOW_Y)]
-R_FLOWS = [(256, FLOW_X), (256, FLOW_Y)]
+PLANE = [("scatter", "plane"), ("exchange", "z"), ("gather", "plane")]
+G_FLOWS = [(G_ROWS // NC, PLANE)]
+R_FLOWS = [(R_ROWS // NC, PLANE)]
 
 
 class Sum:
@@ -328,7 +325,7 @@
     outer = lax.axis_index("outer")
     me = lax.axis_index("inner")
     x, core = outer // NC, lax.rem(outer, NC)
-    y, _ = position(me)
+    y, z = position(me)
 
     loads = [
         pltpu.make_async_copy(features, feat, load_sem.at[0]),
@@ -344,13 +341,22 @@
         pl.semaphore_signal(barrier, inc=1, device_id={"inner": lax.rem(me + d, INNER)}, device_id_type=MESH)
 
     pl.semaphore_signal(barrier, inc=1, device_id={"outer": x * NC + 1 - core}, device_id_type=MESH)
-    for d in range(1, NX):
-        pl.semaphore_signal(barrier, inc=1, device_id={"outer": lax.rem(x + d, NX) * NC + core}, device_id_type=MESH)
+
+    @pl.loop(1, NX)
+    def _(d):
+        @pl.loop(0, NY)
+        def _(row):
+            pl.semaphore_signal(
+                barrier,
+                inc=1,
+                device_id={"outer": lax.rem(x + d, NX) * NC + core, "inner": row * NZ + z},
+                device_id_type=MESH,
+            )
 
     order_picks(small_ref, upper, coded, factors)
     fill_signs(small_ref, flips)
     fill_mixer(factors, flips, mixer)
-    pl.semaphore_wait(barrier, INNER - 1 + 1 + NX - 1)
+    pl.semaphore_wait(barrier, INNER - 1 + 1 + (NX - 1) * NY)
 
     def section(ref, d):
         return ref.at[pl.ds(pl.multiple_of(d * SECTION, SECTION), SECTION)]
@@ -448,6 +454,8 @@
             if p in (i, i + 1):
                 g_own[n * TILE : (n + 1) * TILE, :] = rows[(p - i) * TILE : (p - i + 1) * TILE, (q - i) * TILE : (q - i + 1) * TILE]
     g.step()
+    fill_kron(upper)
+    g.step()
     make(1)
     own = [
         pltpu.make_async_copy(section(out_f, me), section(in_f, me), own_sem.at[0]),
@@ -455,15 +463,11 @@
     ]
     for copy in own:
         copy.start()
-    g.step()
     for i in (0, 2):
         rows = dot(out_f[:, i * TILE : (i + 2) * TILE], out_k[...], TN)
         for n, (p, q) in enumerate(R_BLOCKS):
             if p in (i, i + 1):
                 r_own[n * TILE : (n + 1) * TILE, :] = rows[(p - i) * TILE : (p - i + 1) * TILE, (q - 4) * TILE : (q - 3) * TILE]
-    fill_kron(upper)
-    r.step()
-    g.step()
     r.step()
     g.step()
     r.step()
@@ -472,16 +476,22 @@
     send_rest(0)
     send_rest(1)
     g.step()
-    g.step()
     r.step()
+
+    def unpack(half):
+        for n in range(half * len(G_BLOCKS) // 2, (half + 1) * len(G_BLOCKS) // 2):
+            i, j = G_BLOCKS[n]
+            tile = g_total[n * TILE : (n + 1) * TILE, :]
+            work[i * TILE : (i + 1) * TILE, j * TILE : (j + 1) * TILE] = tile
+            if i != j:
+                work[j * TILE : (j + 1) * TILE, i * TILE : (i + 1) * TILE] = tile.T
+
+    pl.when(core == 0)(functools.partial(unpack, 0))
+    pl.when(core == 1)(functools.partial(unpack, 1))
     g.step()
     assert g.finished
-
-    for n, (i, j) in enumerate(G_BLOCKS):
-        tile = g_total[n * TILE : (n + 1) * TILE, :]
-        work[i * TILE : (i + 1) * TILE, j * TILE : (j + 1) * TILE] = tile
-        if i != j:
-            work[j * TILE : (j + 1) * TILE, i * TILE : (i + 1) * TILE] = tile.T
+    pl.when(core == 0)(functools.partial(unpack, 1))
+    pl.when(core == 1)(functools.partial(unpack, 0))
     targets_at = slice(F, F + K)
     for b in range(F // TILE):
         at = b * TILE
@@ -491,7 +501,6 @@
         if b == 0:
             r.step()
         if b == 1:
-            r.step()
             r.step()
             assert r.finished
             for n, (i, j) in enumerate(R_BLOCKS):

time: 82.6 us -> 82.6 us (level)
  the two profiles are of different devices: /device:TPU:1 before, /device:TPU:29 now
where the time goes in v4:
time: 82.6 us; the launch traced here: 82.4 us
  Pallas kernels  80.8 us (98%)
  between operations  0.83 us (1%)
    pallas_call x1, Pallas kernels, sketch_and_weights(): pl.pallas_call(sketch_kernel, out_shape=(jax.ShapeDtypeStruct((KEEP, F +...  77.5 us
    pallas_call x1, Pallas kernels, predict(): pl.pallas_call(predict_kernel, out_shape=(jax.ShapeDtypeStruct((KEEP, F +...  3.27 us

profile of v4, /device:TPU:29, one launch (start us, length us, event | category | flops | bytes accessed | tf_op | source)
XLA Modules:
  0.0 82.4 jit_solution(17086371515450418941)
XLA Ops:
  0.6 0.8 add_bitcast_fusion.small_ref
  1.4 0.0 copy-start
  1.4 77.5 %sketch.1 = (bf16[1024,768]{1,0:T(8,128)(2,1)S(1)}, f32[512,256]{1,0:T(8,128)S(1)}) custom-call(bf16[4096,512]{1,0:T(8,128)(2,1)} %feat.1, bf16[4096,256]{1,0:T(8,128)(2,1)} %targets.1, s32[48,128]{1,0:T(8,128)S(1)} %add_bitcast_fusion.small_ref), custom_call_target="tpu_custom_call" | custom-call | tf_op jit(solution)/shard_map/sketch/pallas_call | solution.py:529
  78.9 0.0 copy-done
  78.9 3.3 %predict.1 = (bf16[1024,768]{1,0:T(8,128)(2,1)}, f32[512,256]{1,0:T(8,128)}, bf16[4096,256]{1,0:T(8,128)(2,1)}) custom-call(bf16[4096,512]{1,0:T(8,128)(2,1)S(1)} %copy-done, f32[512,256]{1,0:T(8,128)S(1)} %get-tuple-element.5.weights_in, bf16[1024,768]{1,0:T(8,128)(2,1)S(1)} %get-tuple-element.6.sketch_in), custom_call_target="tpu_custom_call" | custom-call | tf_op jit(solution)/shard_map/predict/pallas_call | solution.py:589
Async XLA Ops:
  1.4 77.5 %copy-start = (bf16[4096,512]{1,0:T(8,128)(2,1)S(1)}, bf16[4096,512]{1,0:T(8,128)(2,1)}, u32[]{:S(2)}) copy-start(bf16[4096,512]{1,0:T(8,128)(2,1)} %feat.1) | copy-start | bytes 12582916

commit v5 on v4

--- a/solution.py
+++ b/solution.py
@@ -20,7 +20,6 @@
 R_BLOCKS = [(i, j) for i in range(4) for j in range(4, 6)]
 G_ROWS = TILE * len(G_BLOCKS)
 R_ROWS = TILE * len(R_BLOCKS)
-HIGHEST = lax.Precision.HIGHEST
 MESH = pl.DeviceIdType.MESH
 
 NN = (((1,), (0,)), ((), ()))
@@ -265,6 +264,19 @@
     return shapes, count
 
 
+def thirds(a):
+    high = a.astype(jnp.bfloat16)
+    rest = a - high.astype(jnp.float32)
+    middle = rest.astype(jnp.bfloat16)
+    return high, middle, (rest - middle.astype(jnp.float32)).astype(jnp.bfloat16)
+
+
+def dot_exact(a, b):
+    ah, am, al = thirds(a)
+    bh, bm, bl = thirds(b)
+    return dot(jnp.concatenate([ah, ah, am, am, ah, al], 1), jnp.concatenate([bh, bm, bh, bm, bl, bh], 0))
+
+
 def invert(block):
     lane = iota((8, TILE), 1)
     sub = iota((8, TILE), 0)
@@ -283,11 +295,11 @@
         for s in range(8):
             over = 1.0 / down(cols[s], s)
             mult = jnp.where(sub == s, 0.0, cols[s])
-            row = jnp.where(lane == base + s, 1.0, down(now, s)) * over
-            now = jnp.where(sub == s, row, jnp.where(lane == base + s, 0.0, now) - mult * row)
             for j in range(s + 1, 8):
                 pivot = down(cols[j], s) * over
                 cols[j] = jnp.where(sub == s, pivot, cols[j] - mult * pivot)
+            row = jnp.where(lane == base + s, 1.0, down(now, s)) * over
+            now = jnp.where(sub == s, row, jnp.where(lane == base + s, 0.0, now) - mult * row)
         rows = [down(now, j) for j in range(8)]
         panel = (lane >= base) & (lane < base + 8)
         new = []
@@ -312,7 +324,7 @@
             kron[q * TILE : (q + 1) * TILE, p * TILE : (p + 1) * TILE] = tiles[(q & p).bit_count() & 1]
 
 
-EARLY = {(0, 0), (0, 1)}
+EARLY = {(0, 0)}
 
 
 def sketch_kernel(
@@ -435,11 +447,11 @@
 
     def eliminate(b, columns):
         at = b * TILE
-        pivot = dot(inverse[b], work[at : at + TILE, columns], precision=HIGHEST)
+        pivot = dot_exact(inverse[b], work[at : at + TILE, columns])
         for first, last in ((0, at), (at + TILE, F)):
             if first < last:
-                work[first:last, columns] = work[first:last, columns] - dot(
-                    work[first:last, at : at + TILE], pivot, precision=HIGHEST
+                work[first:last, columns] = work[first:last, columns] - dot_exact(
+                    work[first:last, at : at + TILE], pivot
                 )
         work[at : at + TILE, columns] = pivot
 

time: 82.6 us -> 81.2 us (0.983)
  the two profiles are of different devices: /device:TPU:29 before, /device:TPU:1 now
where the time goes in v5:
time: 81.2 us; the launch traced here: 81 us
  Pallas kernels  79.4 us (98%)
  between operations  0.83 us (1%)
    pallas_call x1, Pallas kernels, sketch_and_weights(): pl.pallas_call(sketch_kernel, out_shape=(jax.ShapeDtypeStruct((KEEP, F +...  76.1 us
    pallas_call x1, Pallas kernels, predict(): pl.pallas_call(predict_kernel, out_shape=(jax.ShapeDtypeStruct((KEEP, F +...  3.27 us

profile of v5, /device:TPU:1, one launch (start us, length us, event | category | flops | bytes accessed | tf_op | source)
XLA Modules:
  0.0 81.0 jit_solution(8896719824905596274)
XLA Ops:
  0.6 0.8 add_bitcast_fusion.small_ref
  1.4 0.0 copy-start
  1.4 76.1 %sketch.1 = (bf16[1024,768]{1,0:T(8,128)(2,1)S(1)}, f32[512,256]{1,0:T(8,128)S(1)}) custom-call(bf16[4096,512]{1,0:T(8,128)(2,1)} %feat.1, bf16[4096,256]{1,0:T(8,128)(2,1)} %targets.1, s32[48,128]{1,0:T(8,128)S(1)} %add_bitcast_fusion.small_ref), custom_call_target="tpu_custom_call" | custom-call | tf_op jit(solution)/shard_map/sketch/pallas_call | solution.py:541
  77.5 0.0 copy-done
  77.5 3.3 %predict.1 = (bf16[1024,768]{1,0:T(8,128)(2,1)}, f32[512,256]{1,0:T(8,128)}, bf16[4096,256]{1,0:T(8,128)(2,1)}) custom-call(bf16[4096,512]{1,0:T(8,128)(2,1)S(1)} %copy-done, f32[512,256]{1,0:T(8,128)S(1)} %get-tuple-element.5.weights_in, bf16[1024,768]{1,0:T(8,128)(2,1)S(1)} %get-tuple-element.6.sketch_in), custom_call_target="tpu_custom_call" | custom-call | tf_op jit(solution)/shard_map/predict/pallas_call | solution.py:601
Async XLA Ops:
  1.4 76.2 %copy-start = (bf16[4096,512]{1,0:T(8,128)(2,1)S(1)}, bf16[4096,512]{1,0:T(8,128)(2,1)}, u32[]{:S(2)}) copy-start(bf16[4096,512]{1,0:T(8,128)(2,1)} %feat.1) | copy-start | bytes 12582916

commit v6 on v5

--- a/solution.py
+++ b/solution.py
@@ -520,12 +520,10 @@
             eliminate(0, targets_at)
         if b:
             eliminate(b, targets_at)
-        if b == 2:
-            arrive(0)
-            mix(0)
     weights_ref[...] = work[:, targets_at]
-    arrive(1)
-    mix(1)
+    for kind in (0, 1):
+        arrive(kind)
+        mix(kind)
     store = pltpu.make_async_copy(sketch, sketch_hbm, store_sem)
     store.start()
     store.wait()

time: 81.2 us -> 80.8 us (level)
  no operation moved by 1% of the time
where the time goes in v6:
time: 80.8 us; the launch traced here: 80.6 us
  Pallas kernels  79 us (98%)
  between operations  0.83 us (1%)
    pallas_call x1, Pallas kernels, sketch_and_weights(): pl.pallas_call(sketch_kernel, out_shape=(jax.ShapeDtypeStruct((KEEP, F +...  75.8 us
    pallas_call x1, Pallas kernels, predict(): pl.pallas_call(predict_kernel, out_shape=(jax.ShapeDtypeStruct((KEEP, F +...  3.27 us

profile of v6, /device:TPU:1, one launch (start us, length us, event | category | flops | bytes accessed | tf_op | source)
XLA Modules:
  0.0 80.6 jit_solution(11039847633803162197)
XLA Ops:
  0.6 0.8 add_bitcast_fusion.small_ref
  1.4 0.0 copy-start
  1.4 75.8 %sketch.1 = (bf16[1024,768]{1,0:T(8,128)(2,1)S(1)}, f32[512,256]{1,0:T(8,128)S(1)}) custom-call(bf16[4096,512]{1,0:T(8,128)(2,1)} %feat.1, bf16[4096,256]{1,0:T(8,128)(2,1)} %targets.1, s32[48,128]{1,0:T(8,128)S(1)} %add_bitcast_fusion.small_ref), custom_call_target="tpu_custom_call" | custom-call | tf_op jit(solution)/shard_map/sketch/pallas_call | solution.py:539
  77.1 0.0 copy-done
  77.2 3.3 %predict.1 = (bf16[1024,768]{1,0:T(8,128)(2,1)}, f32[512,256]{1,0:T(8,128)}, bf16[4096,256]{1,0:T(8,128)(2,1)}) custom-call(bf16[4096,512]{1,0:T(8,128)(2,1)S(1)} %copy-done, f32[512,256]{1,0:T(8,128)S(1)} %get-tuple-element.5.weights_in, bf16[1024,768]{1,0:T(8,128)(2,1)S(1)} %get-tuple-element.6.sketch_in), custom_call_target="tpu_custom_call" | custom-call | tf_op jit(solution)/shard_map/predict/pallas_call | solution.py:599
Async XLA Ops:
  1.4 75.8 %copy-start = (bf16[4096,512]{1,0:T(8,128)(2,1)S(1)}, bf16[4096,512]{1,0:T(8,128)(2,1)}, u32[]{:S(2)}) copy-start(bf16[4096,512]{1,0:T(8,128)(2,1)} %feat.1) | copy-start | bytes 12582916
